TPU v7x, 128 devices: a whole 4x4x4 slice. The times are simulated.
128 devices in a mesh: row: 8 (over y, z_hi), col: 16 (over x, z_lo, core).
Axes of the slice: x: 4, y: 4, z: 4 (z_hi: 2, z_lo: 2; z = z_hi * 2 + z_lo), core: 2. Of those that a mesh axis runs over, the one named last changes fastest.
Arguments:
- integrals: bfloat16 [8192, 8192], P('row', 'col'), may hold values from -0.0625 to 0.0625
- amplitudes: bfloat16 [8192, 8192], P('row', 'col'), may hold values from -6 to 6
- integral_tiles: int32 [64, 64], P('row', 'col'), may hold values 0 or 1
- amplitude_tiles: int32 [64, 64], P('row', 'col'), may hold values 0 or 1
- targets: int32 [64, 64], P('row', 'col'), may hold values from 0 to 511, as said below
Outputs:
- owned: bfloat16 [8, 512, 128, 128], P('row', 'col')
Inputs may be any that keep to these rules, and one draw needn't show every extreme that they name: Within each mesh row the targets of the row's tiles are a permutation of 0 to 511. The tiles of one device go to at most 3 slots of any one block of 32 slots, and to exactly 3 slots of some block, in every row.
All inputs are finite; a program needn't handle non-finite values. No bound on the sum of `integral_tiles` or of `amplitude_tiles` on one device may be relied on, other than what follows from the above.
Results may differ from a plain program's by a relative error of at most 0.001.
Values may be sent and summed in bfloat16 or wider, within the bound.
A program may use at most 128 MiB of HBM per device.

v0:
```python
import jax
import jax.numpy as jnp
from jax import lax
from jax.sharding import PartitionSpec as P


def expand_mask(tiles, like, tile_size):
    return jnp.repeat(jnp.repeat(tiles, tile_size, axis=0), tile_size, axis=1).astype(like.dtype)


def on_device(integrals, amplitudes, integral_tiles, amplitude_tiles, targets):
    tile_size = integrals.shape[0] // integral_tiles.shape[0]
    masked_integrals = integrals * expand_mask(integral_tiles, integrals, tile_size)
    masked_amplitudes = amplitudes * expand_mask(amplitude_tiles, amplitudes, tile_size)
    all_amplitudes = lax.all_gather(masked_amplitudes, "row", axis=0, tiled=True)
    ladder = jnp.dot(
        lax.all_gather(masked_integrals, "col", axis=1, tiled=True),
        all_amplitudes,
        preferred_element_type=jnp.float32,
    )
    ladder = ladder.astype(jnp.bfloat16)
    row_tiles, col_tiles = targets.shape
    tiles_dev = row_tiles * col_tiles
    pieces = ladder.reshape(row_tiles, tile_size, col_tiles, tile_size).transpose(0, 2, 1, 3)
    pieces = pieces.reshape(tiles_dev, tile_size, tile_size)
    col_count = lax.axis_size("col")
    capacity = tiles_dev // col_count + 1
    flat_targets = targets.reshape(tiles_dev)
    target_col = flat_targets // tiles_dev
    target_slot = flat_targets % tiles_dev
    indices = jnp.arange(tiles_dev, dtype=jnp.int32)
    same_target = target_col[:, None] == target_col[None, :]
    earlier = indices[None, :] < indices[:, None]
    bucket_rank = jnp.sum((same_target & earlier).astype(jnp.int32), axis=1)
    position = target_col * capacity + bucket_rank
    outgoing = (
        jnp.zeros((col_count * capacity, tile_size, tile_size), jnp.bfloat16)
        .at[position]
        .set(pieces)
    )
    labels = jnp.full((col_count * capacity,), tiles_dev, jnp.int32).at[position].set(target_slot)
    outgoing = outgoing.reshape(col_count, capacity, tile_size, tile_size)
    labels = labels.reshape(col_count, capacity)
    arrived, arrived_labels = (
        lax.all_to_all(outgoing, "col", split_axis=0, concat_axis=0, tiled=True),
        lax.all_to_all(labels, "col", split_axis=0, concat_axis=0, tiled=True),
    )
    owned = jnp.zeros((tiles_dev, tile_size, tile_size), jnp.bfloat16)
    owned = owned.at[arrived_labels.reshape(-1)].set(
        arrived.reshape(-1, tile_size, tile_size), mode="drop"
    )
    return owned[None]


def solution(mesh):
    in_specs = (P("row", "col"), P("row", "col"), P("row", "col"), P("row", "col"), P("row", "col"))
    out_specs = P("row", "col", None, None)
    return jax.shard_map(
        on_device, mesh=mesh, in_specs=in_specs, out_specs=out_specs, check_vma=False
    )
```

profile of v0, /device:TPU:1, one launch (start us, length us, event | category | flops | bytes accessed | tf_op | source)
XLA Modules:
  0.0 273.9 jit_solution(9856742204747584902)
XLA Ops:
  6.5 0.8 convert_element_type.32
  7.3 0.1 copy.25
  7.5 2.9 %broadcast_in_dim.33 = bf16[1024,4,128]{2,1,0:T(4,128)(2,1)S(1)} broadcast(bf16[1024,4]{1,0:T(8,128)(2,1)S(1)} %bitcast.32), dimensions={0,1} | broadcast | bytes 1056768 | tf_op jit(solution)/shard_map/broadcast_in_dim | solution.py:8
  10.4 1.2 bitcast_multiply_fusion
  11.6 0.0 all-gather.5.cloned.1.call-update
  11.7 0.0 all-gather.3.cloned.1.call-start
  11.7 0.1 copy.24
  11.9 2.9 %broadcast_in_dim.31 = bf16[1024,4,128]{2,1,0:T(4,128)(2,1)S(1)} broadcast(bf16[1024,4]{1,0:T(8,128)(2,1)S(1)} %bitcast.33), dimensions={0,1} | broadcast | bytes 1056768 | tf_op jit(solution)/shard_map/broadcast_in_dim | solution.py:8
  14.8 1.1 bitcast_multiply_fusion.1
  16.0 0.0 all-gather.3.cloned.1.call-update
  16.0 0.1 copy.21
  16.1 0.1 reshape.188
  16.2 0.1 reshape.187
  16.3 0.2 convert_reduce_fusion
  16.5 0.7 scatter_custom_fusion
  17.2 0.7 all_to_all.9
  17.8 7.2 %all-to-all-start = ((s32[16,1,3]{2,1,0:T(1,128)}), s32[16,1,3]{2,1,0:T(1,128)S(1)}, u32[]{:S(2)}, u32[]{:S(2)}) async-start(s32[16,1,3]{2,1,0:T(1,128)} %bitcast.2), calls=%async_computation | async-start | bytes 16384 | tf_op jit(solution)/shard_map/all_to_all | solution.py:46
  25.0 98.6 %all-gather.5.cloned.1.call-done = bf16[8192,512]{1,0:T(8,128)(2,1)} async-done(((bf16[1024,512]{1,0:T(8,128)(2,1)}), bf16[8192,512]{1,0:T(8,128)(2,1)}) %all-gather.5.cloned.1.call-update) | async-done | bytes 8388624 | tf_op jit(solution)/shard_map/all_gather | solution.py:15
  123.6 91.8 %all-gather.3.cloned.1.call-done = bf16[1024,8192]{1,0:T(8,128)(2,1)} async-done(((bf16[1024,512]{1,0:T(8,128)(2,1)}), bf16[1024,8192]{1,0:T(8,128)(2,1)}) %all-gather.3.cloned.1.call-update) | async-done | bytes 16777232 | tf_op jit(solution)/shard_map/all_gather | solution.py:17
  215.5 14.8 %convolution_convert_fusion = bf16[1024,512]{1,0:T(8,128)(2,1)S(1)} fusion(bf16[1024,8192]{1,0:T(8,128)(2,1)} %all-gather.3.cloned.1.call-done, bf16[8192,512]{1,0:T(8,128)(2,1)} %all-gather.5.cloned.1.call-done), kind=kOutput, calls=%fused_computation.3 | convolution fusion | flops 8590458880 | bytes 26214400 | tf_op jit(solution)/shard_map/dot_general | solution.py:16
  230.2 0.3 reshape.190
  230.5 0.2 copy.26
  230.8 1.5 broadcast_in_dim.29
  232.3 4.7 %scatter_fusion = bf16[48,128,128]{2,1,0:T(8,128)(2,1)} fusion(bf16[48,128,128]{2,1,0:T(8,128)(2,1)} %broadcast_in_dim.29, s32[32]{0:T(128)S(1)} %fusion.1, bf16[32,128,128]{2,1,0:T(8,128)(2,1)S(1)} %bitcast.31), kind=kCustom, calls=%fused_computation.1 | custom fusion | bytes 3145856 | tf_op jit(solution)/shard_map/scatter | solution.py:39
  237.0 5.2 %all-to-all-start.1 = ((bf16[16,3,128,128]{3,2,1,0:T(8,128)(2,1)}), bf16[16,3,128,128]{3,2,1,0:T(8,128)(2,1)S(1)}, u32[]{:S(2)}, u32[]{:S(2)}) async-start(bf16[16,3,128,128]{3,2,1,0:T(8,128)(2,1)} %bitcast.8), calls=%async_computation.1 | async-start | bytes 3145728 | tf_op jit(solution)/shard_map/all_to_all | solution.py:45
  242.2 0.5 broadcast.173
  242.7 0.7 reduce.3
  243.4 0.1 reshape.189
  243.5 20.0 %all-to-all-done.1 = bf16[16,3,128,128]{3,2,1,0:T(8,128)(2,1)S(1)} async-done(((bf16[16,3,128,128]{3,2,1,0:T(8,128)(2,1)}), bf16[16,3,128,128]{3,2,1,0:T(8,128)(2,1)S(1)}, u32[]{:S(2)}, u32[]{:S(2)}) %all-to-all-start.1) | async-done | bytes 1572896 | tf_op jit(solution)/shard_map/all_to_all | solution.py:45
  263.5 0.2 broadcast_in_dim.28
  263.7 2.4 scatter_fusion.1
  266.1 1.0 copy-done
  (17 shorter events, 0.1 us)
Async XLA Ops:
  6.5 3.9 %copy-start.1 = (bf16[1024,512]{1,0:T(8,128)(2,1)S(1)}, bf16[1024,512]{1,0:T(8,128)(2,1)}, u32[]{:S(2)}) copy-start(bf16[1024,512]{1,0:T(8,128)(2,1)} %param.6) | copy-start | bytes 3145732
  6.5 117.1 %all-gather.5.cloned.1.call-start = ((), (), s32[]{:S(2)}) async-start(), calls=%async_computation.3 | async-start | bytes 9437184 | tf_op jit(solution)/shard_map/all_gather | solution.py:15
  10.4 1.3 copy-start.4
  11.6 3.2 %copy-start.2 = (bf16[1024,512]{1,0:T(8,128)(2,1)S(1)}, bf16[1024,512]{1,0:T(8,128)(2,1)}, u32[]{:S(2)}) copy-start(bf16[1024,512]{1,0:T(8,128)(2,1)} %param.5) | copy-start | bytes 3145732
  11.7 203.8 %all-gather.3.cloned.1.call-start = ((), (), s32[]{:S(2)}) async-start(), calls=%async_computation.2 | async-start | bytes 17825792 | tf_op jit(solution)/shard_map/all_gather | solution.py:17
  14.8 1.2 copy-start.3
  17.8 219.2 %all-to-all-start = ((s32[16,1,3]{2,1,0:T(1,128)}), s32[16,1,3]{2,1,0:T(1,128)S(1)}, u32[]{:S(2)}, u32[]{:S(2)}) async-start(s32[16,1,3]{2,1,0:T(1,128)} %bitcast.2), calls=%async_computation | async-start | bytes 16384 | tf_op jit(solution)/shard_map/all_to_all | solution.py:46
  237.0 26.5 %all-to-all-start.1 = ((bf16[16,3,128,128]{3,2,1,0:T(8,128)(2,1)}), bf16[16,3,128,128]{3,2,1,0:T(8,128)(2,1)S(1)}, u32[]{:S(2)}, u32[]{:S(2)}) async-start(bf16[16,3,128,128]{3,2,1,0:T(8,128)(2,1)} %bitcast.8), calls=%async_computation.1 | async-start | bytes 3145728 | tf_op jit(solution)/shard_map/all_to_all | solution.py:45
  266.1 1.0 copy-start
Sparse Core Ops, SparseCore 0:
  11.8 111.8 all-gather.4
  125.3 90.1 all-gather.2
where the time goes:
time: 274 us
  waiting for transfers between devices  211 us (77%)
  local copies, waits for them, and re-layouts  18.7 us (7%)
  matrix products  14.8 us (5%)
  between operations  13.6 us (5%)
  starting transfers between devices  12.4 us (5%)
  other arithmetic  3.99 us (1%)
    all_gather x1, waiting for transfers between devices, on_device(): lax.all_gather(masked_amplitudes, 'row', axis=0, tiled=True)  98.6 us
    all_gather x1, waiting for transfers between devices, on_device(): lax.all_gather(masked_integrals, 'col', axis=1, tiled=True)  91.8 us
    all_to_all x1, waiting for transfers between devices, on_device(): lax.all_to_all(outgoing, 'col', split_axis=0, concat_axis=0, tiled=True)  20 us
    dot_general x1, matrix products, on_device(): jnp.dot(lax.all_gather(masked_integrals, 'col', axis=1, tiled=True), all_...  14.8 us
    all_to_all x1, starting transfers between devices, on_device(): lax.all_to_all(labels, 'col', split_axis=0, concat_axis=0, tiled=True)  7.17 us
    broadcast_in_dim x2, local copies, waits for them, and re-layouts, expand_mask(): jnp.repeat(jnp.repeat(tiles, tile_size, axis=0), tile_size, axis=1)  5.89 us
  transfers between devices with their start and end apart: 4, of which 3 were waited for; matrix products, arithmetic and copies ran while one was open for 10% of the time, Pallas kernels for 0%

commit v1 on v0

v1 whole, which is shorter than its diff:
```python
import functools

import jax
import jax.numpy as jnp
from jax import lax
from jax.experimental import pallas as pl
from jax.experimental.pallas import tpu as pltpu
from jax.sharding import PartitionSpec as P

MESH = pl.DeviceIdType.MESH
T = 128
CAP = 3
PIECES = 4
PARTS = 2


class Sems:
    def __init__(self, ref):
        self.ref, self.used = ref, 0

    def take(self):
        self.used += 1
        return self.ref.at[self.used - 1]


def kernel(
    a_ref, b_ref, a_tiles, b_tiles, targets, out_ref,
    a_all, b_all, total, tiles, packed_parts, arrived_parts, label_out, label_in, table, table_s,
    send_ref, recv_a, recv_s, recv_b, recv_l, recv_d, local_sem,
):
    row, col = lax.axis_index("row"), lax.axis_index("col")
    y, zh = row // 2, row % 2
    x, zl, core = col // 4, (col // 2) % 2, col % 2
    sends = Sems(send_ref)
    started = []

    def col_of(dx, dv, dc):
        return lax.rem(x + dx + 4, 4) * 4 + lax.rem(zl + dv, 2) * 2 + lax.rem(core + dc, 2)

    def row_of(dy, dv):
        return lax.rem(y + dy + 4, 4) * 2 + lax.rem(zh + dv, 2)

    def send(src, dst, recv_sem, device):
        copy = pltpu.make_async_remote_copy(
            src_ref=src, dst_ref=dst, send_sem=sends.take(), recv_sem=recv_sem,
            device_id=device, device_id_type=MESH,
        )
        copy.start()
        started.append(copy)

    def landed(dst, recv_sem, device):
        pltpu.make_async_remote_copy(
            src_ref=dst, dst_ref=dst, send_sem=send_ref.at[0], recv_sem=recv_sem,
            device_id=device, device_id_type=MESH,
        ).wait_recv()

    barrier = pltpu.get_barrier_semaphore()
    peers = [(row, lax.rem(col + d, 16)) for d in range(1, 16)]
    peers += [(row_of(1, 0), col), (row_of(-1, 0), col), (row_of(0, 1), col)]
    for peer in peers:
        pl.semaphore_signal(barrier, inc=1, device_id=peer, device_id_type=MESH)

    rows_p = 8 // PIECES

    def mask(src, tile_flags, dst, p):
        for i in range(p * rows_p, (p + 1) * rows_p):
            for j in range(4):
                flag = tile_flags[i, j].astype(jnp.float32)
                block = src[pl.ds(i * T, T), pl.ds(j * T, T)].astype(jnp.float32) * flag
                dst[i, :, pl.ds(j * T, T)] = block.astype(jnp.bfloat16)

    mine_a = a_all.at[col]
    mine_b = b_all.at[row]
    mask(a_ref, a_tiles, mine_a, 0)
    mask(b_ref, b_tiles, mine_b, 0)
    pl.semaphore_wait(barrier, len(peers))

    def a_piece(dx, dv, dc, p):
        return a_all.at[col_of(-dx, dv, dc), pl.ds(p * rows_p, rows_p)]

    def b_piece(dy, dv, p):
        return b_all.at[row_of(-dy, dv), pl.ds(p * rows_p, rows_p)]

    def send_a(dx, dv, p, how):
        piece = a_piece(dx, dv, 0, p)
        if how == "right":
            send(piece, piece, recv_a.at[dx + 1, dv, p], (row, col_of(1, 0, 0)))
        elif how == "left":
            send(piece, piece, recv_a.at[(dx + 3) % 4, dv, p], (row, col_of(-1, 0, 0)))
        elif how == "z":
            send(piece, piece, recv_a.at[dx, 1 - dv, p], (row, col_of(0, 1, 0)))
        else:
            send(piece, piece, recv_s.at[dx, dv, p], (row, col_of(0, 0, 1)))

    def send_b(dy, dv, p, how):
        piece = b_piece(dy, dv, p)
        if how == "right":
            send(piece, piece, recv_b.at[dy + 1, dv, p], (row_of(1, 0), col))
        elif how == "left":
            send(piece, piece, recv_b.at[(dy + 3) % 4, dv, p], (row_of(-1, 0), col))
        else:
            send(piece, piece, recv_b.at[dy, 1 - dv, p], (row_of(0, 1), col))

    def got_a(dx, dv, p):
        landed(a_piece(dx, dv, 0, p), recv_a.at[dx, dv, p], (row, col_of(0, 1, 0)))

    def got_s(dx, dv, p):
        landed(a_piece(dx, dv, 1, p), recv_s.at[dx, dv, p], (row, col_of(0, 0, 1)))

    def got_b(dy, dv, p):
        landed(b_piece(dy, dv, p), recv_b.at[dy, dv, p], (row_of(0, 1), col))

    for p in range(PIECES):
        if p:
            mask(a_ref, a_tiles, mine_a, p)
        for how in ("z", "left", "right"):
            send_a(0, 0, p, how)
        if p:
            mask(b_ref, b_tiles, mine_b, p)
        for how in ("z", "left", "right"):
            send_b(0, 0, p, how)
    for p in range(PIECES):
        send_a(0, 0, p, "core")

    lane = lax.broadcasted_iota(jnp.int32, (8, 128), 1)
    lane16 = lax.broadcasted_iota(jnp.int32, (16, 8, 128), 2)
    owner16 = lax.broadcasted_iota(jnp.int32, (16, 8, 128), 0)

    def place(t, carry):
        source, label = carry
        target = targets[t // 4, lax.rem(t, 4)]
        owner, slot = target // 32, lax.rem(target, 32)

        def count(s, rank):
            same = targets[s // 4, lax.rem(s, 4)] // 32 == owner
            return rank + jnp.where(same, 1, 0)

        rank = lax.fori_loop(0, t, count, jnp.int32(0))
        source = jnp.where(lane == owner * CAP + rank, t, source)
        label = jnp.where((owner16 == owner) & (lane16 == slot), col * CAP + rank + 1, label)
        return source, label

    source, label = lax.fori_loop(
        0, 32, place, (jnp.zeros((8, 128), jnp.int32), jnp.zeros((16, 8, 128), jnp.int32))
    )
    label_out[...] = label
    for d in range(1, 16):
        peer = lax.rem(col + d, 16)
        send(label_out.at[peer], label_in.at[col], recv_l.at[d], (row, peer))
    table[0] = source
    copy = pltpu.make_async_copy(table.at[0], table_s.at[0], local_sem.at[0])
    copy.start()
    copy.wait()
    label_in[col] = label_out[col]

    half = PIECES // 2
    for dv in (0, 1):
        for p in range(PIECES):
            got_a(1, dv, p)
            if p < half:
                send_a(1, dv, p, "right")
            got_a(3, dv, p)
            if p >= half:
                send_a(3, dv, p, "left")
            got_b(1, dv, p)
            if p < half:
                send_b(1, dv, p, "right")
            got_b(3, dv, p)
            if p >= half:
                send_b(3, dv, p, "left")
            if dv == 0:
                got_a(0, 1, p)
                send_a(0, 1, p, "left")
                send_a(0, 1, p, "right")
                got_b(0, 1, p)
                send_b(0, 1, p, "left")
                send_b(0, 1, p, "right")
                send_a(0, 1, p, "core")
            send_a(1, dv, p, "core")
            send_a(3, dv, p, "core")

    odd = lax.rem(x + y, 2)
    first = lax.rem(x + 1 - odd, 4)
    second = lax.rem((1 - odd) * (x + 3) + odd * y, 4)
    third = lax.rem(x + 2, 4)
    fourth = lax.rem((1 - odd) * x + odd * (y + 2), 4)

    size = T // PARTS

    def dots(u, part):
        result = None
        for v in range(2):
            for c in range(2):
                left = a_all[u * 4 + v * 2 + c, :, pl.ds(part * size, size), :].reshape(8 * size, 4 * T)
                right = b_all[u * 2 + v, pl.ds(c * 4, 4)].reshape(4 * T, 4 * T)
                term = jnp.dot(left, right, preferred_element_type=jnp.float32)
                result = term if result is None else result + term
        return result

    for dv in (0, 1):
        for dx in (0, 1, 3):
            for p in range(PIECES):
                got_s(dx, dv, p)

    for dv in (0, 1):
        for p in range(PIECES):
            got_a(2, dv, p)
            send_a(2, dv, p, "core")
            got_b(2, dv, p)

    for d in range(1, 16):
        peer = lax.rem(col - d + 16, 16)
        landed(label_in.at[peer], recv_l.at[d], (row, peer))
    table[1] = jnp.sum(label_in[...], axis=0) - 1
    copy = pltpu.make_async_copy(table.at[1], table_s.at[1], local_sem.at[1])
    copy.start()
    copy.wait()

    for dv in (0, 1):
        for p in range(PIECES):
            got_s(2, dv, p)

    for part in range(PARTS):
        total[part] = dots(first, part)
        total[part] += dots(second, part)
        total[part] += dots(third, part)
        ladder = (total[part] + dots(fourth, part)).astype(jnp.bfloat16)
        ladder = ladder.reshape(8, size, 4 * T)
        for i in range(8):
            for j in range(4):
                tiles[part, i * 4 + j] = ladder[i, :, j * T:(j + 1) * T]

        def pack(k, carry):
            packed_parts[part][k] = tiles[part, jnp.clip(table_s[0, 0, k], 0, 31)]
            return carry

        lax.fori_loop(0, 16 * CAP, pack, 0)
        for d in range(1, 16):
            peer = lax.rem(col + d, 16)
            send(
                packed_parts[part].at[pl.ds(peer * CAP, CAP)], arrived_parts[part].at[pl.ds(col * CAP, CAP)],
                recv_d.at[part, d], (row, peer),
            )
        for k in range(CAP):
            arrived_parts[part][col * CAP + k] = packed_parts[part][col * CAP + k]

    for part in range(PARTS):
        for d in range(1, 16):
            peer = lax.rem(col - d + 16, 16)
            landed(arrived_parts[part].at[pl.ds(peer * CAP, CAP)], recv_d.at[part, d], (row, peer))

        def unpack(k, carry):
            out_ref[0, k, pl.ds(part * size, size), :] = arrived_parts[part][jnp.clip(table_s[1, 0, k], 0, 16 * CAP - 1)]
            return carry

        lax.fori_loop(0, 32, unpack, 0)
    for copy in started:
        copy.wait_send()


def on_device(integrals, amplitudes, integral_tiles, amplitude_tiles, targets):
    bf16 = jnp.bfloat16
    size = T // PARTS
    vmem, smem = pl.BlockSpec(memory_space=pltpu.VMEM), pl.BlockSpec(memory_space=pltpu.SMEM)
    dma = pltpu.SemaphoreType.DMA
    return pl.pallas_call(
        kernel,
        out_shape=jax.ShapeDtypeStruct((1, 32, T, T), bf16),
        in_specs=[vmem, vmem, smem, smem, smem],
        out_specs=vmem,
        scratch_shapes=[
            pltpu.VMEM((16, 8, T, 4 * T), bf16),
            pltpu.VMEM((8, 8, T, 4 * T), bf16),
            pltpu.VMEM((PARTS, 8 * size, 4 * T), jnp.float32),
            pltpu.VMEM((PARTS, 32, size, T), bf16),
            [pltpu.VMEM((16 * CAP, size, T), bf16) for _ in range(PARTS)],
            [pltpu.VMEM((16 * CAP, size, T), bf16) for _ in range(PARTS)],
            pltpu.VMEM((16, 8, 128), jnp.int32),
            pltpu.VMEM((16, 8, 128), jnp.int32),
            pltpu.VMEM((2, 8, 128), jnp.int32),
            pltpu.SMEM((2, 8, 128), jnp.int32),
            dma((256,)),
            dma((4, 2, PIECES)),
            dma((4, 2, PIECES)),
            dma((4, 2, PIECES)),
            dma((16,)),
            dma((PARTS, 16)),
            dma((2,)),
        ],
        compiler_params=pltpu.CompilerParams(
            collective_id=0, has_side_effects=True, vmem_limit_bytes=56 * 2**20
        ),
        cost_estimate=pl.CostEstimate(
            flops=2 * 1024 * 512 * 8192, bytes_accessed=3 * 2**20, transcendentals=0
        ),
    )(integrals, amplitudes, integral_tiles, amplitude_tiles, targets)


def solution(mesh):
    spec = P("row", "col")
    return jax.shard_map(
        on_device, mesh=mesh, in_specs=(spec,) * 5, out_specs=P("row", "col", None, None), check_vma=False
    )
```

time: 274 us -> 115 us (0.42)
  waiting for transfers between devices: 211 us -> 0 us
  Pallas kernels: 0 us -> 109 us
  matrix products: 14.8 us -> 0 us
  local copies, waits for them, and re-layouts: 18.7 us -> 5.02 us
  between operations: 13.6 us -> 0.01 us
  starting transfers between devices: 12.4 us -> 0 us
  other arithmetic: 3.99 us -> 0 us
    all_gather x2 -> x0, waiting for transfers between devices: 190 us -> none  [the longest x1 98.6 us: on_device(): lax.all_gather(masked_amplitudes, 'row', axis=0, tiled=True)]
    pallas_call x0 -> x1, Pallas kernels: none -> 109 us  [on_device(): pl.pallas_call(kernel, out_shape=jax.ShapeDtypeStruct((1, 32, T, T), bf16...]
    all_to_all x2 -> x0, waiting for transfers between devices: 20 us -> none  [the longest x1 20 us: on_device(): lax.all_to_all(outgoing, 'col', split_axis=0, concat_axis=0, tiled=True)]
    dot_general x1 -> x0, matrix products: 14.8 us -> none  [on_device(): jnp.dot(lax.all_gather(masked_integrals, 'col', axis=1, tiled=True), all_...]
    all_to_all x2 -> x0, starting transfers between devices: 12.3 us -> none  [the longest x1 7.17 us: on_device(): lax.all_to_all(labels, 'col', split_axis=0, concat_axis=0, tiled=True)]
    broadcast_in_dim x6 -> x0, local copies, waits for them, and re-layouts: 7.73 us -> none  [the longest x2 5.89 us: expand_mask(): jnp.repeat(jnp.repeat(tiles, tile_size, axis=0), tile_size, axis=1)]
    scatter x3 -> x0, local copies, waits for them, and re-layouts: 7.71 us -> none  [the longest x1 4.67 us: on_device(): outgoing = jnp.zeros((col_count * capacity, tile_size, tile_size), jnp.bf...]
    unnamed x11 -> x8, local copies, waits for them, and re-layouts: 1.07 us -> 5.02 us
  transfers between devices with their start and end apart: 4 -> 0, of which waited for: 3 -> 0; matrix products, arithmetic and copies ran while one was open for 10% -> 0% of each run, Pallas kernels for 0% -> 0%
where the time goes in v1:
time: 115 us; the launch traced here: 114 us
  Pallas kernels  109 us (95%)
  local copies, waits for them, and re-layouts  5.02 us (4%)
    pallas_call x1, Pallas kernels, on_device(): pl.pallas_call(kernel, out_shape=jax.ShapeDtypeStruct((1, 32, T, T), bf16...  109 us
    unnamed x8, local copies, waits for them, and re-layouts  5.02 us

profile of v1, /device:TPU:1, one launch (start us, length us, event | category | flops | bytes accessed | tf_op | source)
XLA Modules:
  0.0 113.6 jit_solution(9675425289094422003)
XLA Ops:
  0.0 0.0 copy-start
  0.0 1.4 %copy.6.a_tiles = s32[8,4]{1,0:T(8,128)} copy(s32[8,4]{0,1:T(4,128)} %param.7) | data formatting | bytes 256 | tf_op args[2]
  1.4 0.0 copy-done
  1.4 0.0 copy-start.1
  1.4 0.7 copy.7.b_tiles
  2.0 0.0 copy-done.1
  2.0 0.7 copy.8.targets
  2.7 108.6 %shard_map.55 = bf16[1,32,128,128]{3,2,1,0:T(8,128)(2,1)} custom-call(bf16[1024,512]{1,0:T(8,128)(2,1)} %a_ref.1, bf16[1024,512]{1,0:T(8,128)(2,1)} %b_ref.1, s32[8,4]{1,0:T(8,128)} %copy.6.a_tiles, s32[8,4]{1,0:T(8,128)} %copy.7.b_tiles, s32[8,4]{1,0:T(8,128)} %copy.8.targets), custom_call_target="tpu_custom_call" | custom-call | flops 8589934592 | bytes 3145728 | tf_op jit(solution)/shard_map/pallas_call | solution.py:266
  111.3 2.3 %copy.10 = bf16[1,32,128,128]{3,2,1,0:T(8,128)(2,1)} copy(bf16[1,32,128,128]{3,2,1,0:T(8,128)(2,1)} %shard_map.55) | data formatting | bytes 2097152
Async XLA Ops:
  0.0 1.4 %copy-start = (s32[8,4]{0,1:T(4,128)S(1)}, s32[8,4]{0,1:T(4,128)}, u32[]{:S(2)}) copy-start(s32[8,4]{0,1:T(4,128)} %param.8) | copy-start | bytes 388
  1.4 0.7 copy-start.1

commit v2 on v1

v2 whole, which is shorter than its diff:
```python
import functools

import jax
import jax.numpy as jnp
from jax import lax
from jax.experimental import pallas as pl
from jax.experimental.pallas import tpu as pltpu
from jax.sharding import PartitionSpec as P

MESH = pl.DeviceIdType.MESH
T = 128
CAP = 3
PIECES = 4
LATE = 0
GREET_ALL = False
SPREAD = [1, 15, 2, 14, 3, 13, 4, 12, 5, 11, 6, 10, 7, 9, 8]
PARTS = 2


class Sems:
    def __init__(self, ref):
        self.ref, self.used = ref, 0

    def take(self):
        self.used += 1
        return self.ref.at[self.used - 1]


def forwards(steps, dv, p):
    kept = (p < PIECES // 2) != (dv == 1 and PIECES - LATE == p)
    return steps == 1 and kept or steps == 3 and not kept


def arrival_order():
    queues = {(m, way): [] for m in "ab" for way in ("left", "right", "z")}
    left_over, order, now = {key: 0.0 for key in queues}, [], 0.0
    for m in "ab":
        for p in own_order():
            queues[m, "left"].append((3, 0, p))
            queues[m, "right"].append((1, 0, p))
        for p in own_order():
            if p < PIECES - LATE:
                queues[m, "z"].append((0, 1, p))
        for p in range(PIECES - LATE, PIECES):
            queues[m, "z"].append((0, 1, p))
    while any(queues.values()):
        both = queues["a", "z"] and queues["b", "z"]
        for (m, way), queue in queues.items():
            if queue:
                left_over[m, way] += 0.0625 if way == "z" and both else 0.125
        for (m, way), queue in queues.items():
            if queue and left_over[m, way] >= 1.0:
                left_over[m, way] = 0.0
                steps, dv, p = queue.pop(0)
                order.append((m, steps, dv, p))
                for how in onward(steps, dv, p):
                    if how == "z":
                        queues[m, "z"].append((steps, 1 - dv, p))
                    elif how == "right":
                        queues[m, "right"].append((steps + 1, dv, p))
                    else:
                        queues[m, "left"].append(((steps + 3) % 4, dv, p))
    return order


def own_order():
    return [*range(PIECES - LATE, PIECES), *range(PIECES - LATE)]


def onward(steps, dv, p):
    late = p >= PIECES - LATE
    ways = []
    if steps == 0 and dv == 1 and not late:
        ways += ["left", "right"]
    if steps in (1, 3) and not (dv == 1 and late) and forwards(steps, dv, p):
        ways.append("right" if steps == 1 else "left")
    if dv == 0 and late and steps:
        ways.append("z")
    return ways


def kernel(
    a_hbm, b_hbm, a_tiles, b_tiles, targets, arrived, slots_ref,
    a_in, b_in, a_all, b_all, total, tiles, packed_parts, label_out, label_in, table, table_s,
    send_ref, recv_a, recv_s, recv_b, recv_l, recv_d, local_sem,
):
    row, col = lax.axis_index("row"), lax.axis_index("col")
    y, zh = row // 2, row % 2
    x, zl, core = col // 4, (col // 2) % 2, col % 2
    sends = Sems(send_ref)
    started = []

    def col_of(dx, dv, dc):
        return lax.rem(x + dx + 4, 4) * 4 + lax.rem(zl + dv, 2) * 2 + lax.rem(core + dc, 2)

    def row_of(dy, dv):
        return lax.rem(y + dy + 4, 4) * 2 + lax.rem(zh + dv, 2)

    def send(src, dst, recv_sem, device):
        copy = pltpu.make_async_remote_copy(
            src_ref=src, dst_ref=dst, send_sem=sends.take(), recv_sem=recv_sem,
            device_id=device, device_id_type=MESH,
        )
        copy.start()
        started.append(copy)

    def landed(dst, recv_sem, device):
        pltpu.make_async_remote_copy(
            src_ref=dst, dst_ref=dst, send_sem=send_ref.at[0], recv_sem=recv_sem,
            device_id=device, device_id_type=MESH,
        ).wait_recv()

    barrier = pltpu.get_barrier_semaphore()
    if GREET_ALL:
        peers = [(row, lax.rem(col + d, 16)) for d in range(1, 16)]
    else:
        peers = [(row, col_of(1, 0, 0)), (row, col_of(-1, 0, 0)), (row, col_of(0, 1, 0)), (row, col_of(0, 0, 1))]
    peers += [(row_of(1, 0), col), (row_of(-1, 0), col), (row_of(0, 1), col)]
    for peer in peers:
        pl.semaphore_signal(barrier, inc=1, device_id=peer, device_id_type=MESH)

    rows_p = 8 // PIECES
    order = own_order()
    loads = []
    for n, p in enumerate(order):
        rows = pl.ds(p * rows_p * T, rows_p * T)
        loads.append((
            pltpu.make_async_copy(a_hbm.at[rows], a_in.at[rows], local_sem.at[2 + 2 * n]),
            pltpu.make_async_copy(b_hbm.at[rows], b_in.at[rows], local_sem.at[3 + 2 * n]),
        ))
        for load in loads[-1]:
            load.start()

    def mask(src, tile_flags, dst, p):
        for i in range(p * rows_p, (p + 1) * rows_p):
            for j in range(4):
                flag = tile_flags[j, i].astype(jnp.float32)
                block = src[pl.ds(i * T, T), pl.ds(j * T, T)].astype(jnp.float32) * flag
                dst[i, :, pl.ds(j * T, T)] = block.astype(jnp.bfloat16)

    def a_piece(dx, dv, dc, p):
        return a_all.at[col_of(-dx, dv, dc), pl.ds(p * rows_p, rows_p)]

    def b_piece(dy, dv, p):
        return b_all.at[row_of(-dy, dv), pl.ds(p * rows_p, rows_p)]

    def send_a(dx, dv, p, how):
        piece = a_piece(dx, dv, 0, p)
        if how == "right":
            send(piece, piece, recv_a.at[dx + 1, dv, p], (row, col_of(1, 0, 0)))
        elif how == "left":
            send(piece, piece, recv_a.at[(dx + 3) % 4, dv, p], (row, col_of(-1, 0, 0)))
        elif how == "z":
            send(piece, piece, recv_a.at[dx, 1 - dv, p], (row, col_of(0, 1, 0)))
        else:
            send(piece, piece, recv_s.at[dx, dv, p], (row, col_of(0, 0, 1)))

    def send_b(dy, dv, p, how):
        piece = b_piece(dy, dv, p)
        if how == "right":
            send(piece, piece, recv_b.at[dy + 1, dv, p], (row_of(1, 0), col))
        elif how == "left":
            send(piece, piece, recv_b.at[(dy + 3) % 4, dv, p], (row_of(-1, 0), col))
        else:
            send(piece, piece, recv_b.at[dy, 1 - dv, p], (row_of(0, 1), col))

    def got_s(dx, dv, p):
        landed(a_piece(dx, dv, 1, p), recv_s.at[dx, dv, p], (row, col_of(0, 0, 1)))

    mine_a, mine_b = a_all.at[col], b_all.at[row]
    for n, p in enumerate(order):
        late = p >= PIECES - LATE
        for load in loads[n]:
            load.wait()
        mask(a_in, a_tiles, mine_a, p)
        mask(b_in, b_tiles, mine_b, p)
        if n == 0:
            pl.semaphore_wait(barrier, len(peers))
        for one in (send_a, send_b):
            if not late:
                one(0, 0, p, "z")
            one(0, 0, p, "left")
            one(0, 0, p, "right")
    for p in range(PIECES - LATE, PIECES):
        send_a(0, 0, p, "z")
        send_b(0, 0, p, "z")
    for p in order:
        send_a(0, 0, p, "core")

    at_tile = lax.broadcasted_iota(jnp.int32, (32, 128), 0)
    lane = lax.broadcasted_iota(jnp.int32, (32, 128), 1)
    target = jnp.zeros((32, 128), jnp.int32)
    for t in range(32):
        target = jnp.where(at_tile == t, targets[t % 4, t // 4], target)
    owner, slot = target // 32, target % 32
    rank = jnp.zeros((32, 128), jnp.int32)
    for t in range(32):
        rank += jnp.where((at_tile > t) & (owner == targets[t % 4, t // 4] // 32), 1, 0)
    place = owner * CAP + rank
    table[0] = jnp.broadcast_to(
        jnp.sum(jnp.where(place == lane, at_tile, 0), axis=0, keepdims=True), (8, 128)
    )
    for w in range(16):
        here = jnp.where((owner == w) & (slot == lane), col * CAP + rank + 1, 0)
        label_out[w] = jnp.broadcast_to(jnp.sum(here, axis=0, keepdims=True), (8, 128))
    copy = pltpu.make_async_copy(table.at[0], table_s, local_sem.at[0])
    copy.start()
    copy.wait()

    odd = lax.rem(x + y, 2)
    near, far = lax.rem(x + 1, 4), lax.rem(x + 3, 4)
    size = T // PARTS

    def dots(quarter, v, part):
        result = None
        for c in range(2):
            left = a_all[quarter * 4 + v * 2 + c, :, pl.ds(part * size, size), :].reshape(8 * size, 4 * T)
            right = b_all[quarter * 2 + v, pl.ds(c * 4, 4)].reshape(4 * T, 4 * T)
            term = jnp.dot(left, right, preferred_element_type=jnp.float32)
            result = term if result is None else result + term
        return result

    def add_dots(opposite, part):
        def quarters(one, other):
            result = total[part] if opposite else None
            for quarter in (one, other):
                for v in range(2):
                    term = dots(quarter, v, part)
                    result = term if result is None else result + term
            total[part] = result

        @pl.when(odd == 0)
        def _():
            quarters(*((x, lax.rem(x + 2, 4)) if opposite else (near, far)))

        @pl.when(odd == 1)
        def _():
            quarters(*((lax.rem(x + 2, 4), lax.rem(y + 2, 4)) if opposite else (x, y)))

    todo = {(m, steps, dv, p) for m in "abs" for steps in range(4) for dv in range(2) for p in range(PIECES)}
    todo -= {("a", 0, 0, p) for p in range(PIECES)} | {("b", 0, 0, p) for p in range(PIECES)}

    def need(steps, dv):
        for p in range(PIECES):
            if ("s", steps, dv, p) in todo:
                todo.discard(("s", steps, dv, p))
                got_s(steps, dv, p)

    early = False
    for m, steps, dv, p in arrival_order():
        todo.discard((m, steps, dv, p))
        if m == "a":
            landed(a_piece(steps, dv, 0, p), recv_a.at[steps, dv, p], (row, col_of(0, 1, 0)))
        else:
            landed(b_piece(steps, dv, p), recv_b.at[steps, dv, p], (row_of(0, 1), col))
        for how in onward(steps, dv, p):
            (send_a if m == "a" else send_b)(steps, dv, p, how)
        if m == "a":
            send_a(steps, dv, p, "core")
        if not early and not any(n != "s" and d != 2 for n, d, _, _ in todo):
            early = True
            for d in range(1, 16):
                peer = lax.rem(col + d, 16)
                send(label_out.at[peer], label_in.at[col], recv_l.at[d], (row, peer))
            label_in[col] = label_out[col]
            for dx in (0, 1, 3):
                for dv in range(2):
                    need(dx, dv)
            for part in range(PARTS):
                add_dots(False, part)

    for d in range(1, 16):
        peer = lax.rem(col - d + 16, 16)
        landed(label_in.at[peer], recv_l.at[d], (row, peer))
    slots_ref[...] = jnp.clip(jnp.sum(label_in[...], axis=0) - 1, 0, 16 * CAP - 1)

    for dv in range(2):
        need(2, dv)

    stays = []
    for part in range(PARTS):
        add_dots(True, part)
        ladder = total[part].astype(jnp.bfloat16).reshape(8, size, 4 * T)
        for i in range(8):
            for j in range(4):
                tiles[part, i * 4 + j] = ladder[i, :, j * T:(j + 1) * T]

        def pack(k, carry):
            packed_parts[part][k] = tiles[part, jnp.clip(table_s[0, k], 0, 31)]
            return carry

        lax.fori_loop(0, 16 * CAP, pack, 0, unroll=4)
        rows = pl.ds(part * size, size)
        for d in SPREAD:
            peer = lax.rem(col + d, 16)
            send(
                packed_parts[part].at[pl.ds(peer * CAP, CAP)], arrived.at[pl.ds(col * CAP, CAP), rows],
                recv_d.at[part, d], (row, peer),
            )
        stays.append(pltpu.make_async_copy(
            packed_parts[part].at[pl.ds(col * CAP, CAP)], arrived.at[pl.ds(col * CAP, CAP), rows],
            local_sem.at[2 + part],
        ))
        stays[-1].start()

    for part in range(PARTS):
        rows = pl.ds(part * size, size)
        stays[part].wait()
        for d in SPREAD:
            peer = lax.rem(col - d + 16, 16)
            landed(arrived.at[pl.ds(peer * CAP, CAP), rows], recv_d.at[part, d], (row, peer))
    for copy in started:
        copy.wait_send()


def unpack(slots, arrived, owned):
    def one(k, carry):
        owned[0, k] = arrived[slots[0, k]]
        return carry

    lax.fori_loop(0, 32, one, 0, unroll=4)


def on_device(integrals, amplitudes, integral_tiles, amplitude_tiles, targets):
    bf16 = jnp.bfloat16
    size = T // PARTS
    vmem, smem, hbm = (pl.BlockSpec(memory_space=s) for s in (pltpu.VMEM, pltpu.SMEM, pl.ANY))
    dma = pltpu.SemaphoreType.DMA
    arrived, slots = pl.pallas_call(
        kernel,
        out_shape=(
            jax.ShapeDtypeStruct((16 * CAP, T, T), bf16),
            jax.ShapeDtypeStruct((8, 128), jnp.int32),
        ),
        in_specs=[hbm, hbm, smem, smem, smem],
        out_specs=(hbm, vmem),
        scratch_shapes=[
            pltpu.VMEM((8 * T, 4 * T), bf16),
            pltpu.VMEM((8 * T, 4 * T), bf16),
            pltpu.VMEM((16, 8, T, 4 * T), bf16),
            pltpu.VMEM((8, 8, T, 4 * T), bf16),
            pltpu.VMEM((PARTS, 8 * size, 4 * T), jnp.float32),
            pltpu.VMEM((PARTS, 32, size, T), bf16),
            [pltpu.VMEM((16 * CAP, size, T), bf16) for _ in range(PARTS)],
            pltpu.VMEM((16, 8, 128), jnp.int32),
            pltpu.VMEM((16, 8, 128), jnp.int32),
            pltpu.VMEM((1, 8, 128), jnp.int32),
            pltpu.SMEM((8, 128), jnp.int32),
            dma((320,)),
            dma((4, 2, PIECES)),
            dma((4, 2, PIECES)),
            dma((4, 2, PIECES)),
            dma((16,)),
            dma((PARTS, 16)),
            dma((2 + 2 * PIECES,)),
        ],
        compiler_params=pltpu.CompilerParams(
            collective_id=0, has_side_effects=True, vmem_limit_bytes=56 * 2**20
        ),
        cost_estimate=pl.CostEstimate(
            flops=2 * 1024 * 512 * 8192, bytes_accessed=4 * 2**20, transcendentals=0
        ),
    )(integrals, amplitudes, integral_tiles.T, amplitude_tiles.T, targets.T)
    return pl.pallas_call(
        unpack,
        out_shape=jax.ShapeDtypeStruct((1, 32, T, T), bf16),
        in_specs=[smem, vmem],
        out_specs=vmem,
    )(slots, arrived)


def solution(mesh):
    spec = P("row", "col")
    return jax.shard_map(
        on_device, mesh=mesh, in_specs=(spec,) * 5, out_specs=P("row", "col", None, None), check_vma=False
    )
```

time: 115 us -> 112 us (0.974)
  local copies, waits for them, and re-layouts: 5.02 us -> 0 us
  Pallas kernels: 109 us -> 112 us
    unnamed x8 -> x0, local copies, waits for them, and re-layouts: 5.02 us -> none
    pallas_call x1 -> x2, Pallas kernels: 109 us -> 112 us  [the longest x1 109 us: on_device(): pl.pallas_call(kernel, out_shape=(jax.ShapeDtypeStruct((16 * CAP, T, T),...]
where the time goes in v2:
time: 112 us
  Pallas kernels  112 us (100%)
    pallas_call x1, Pallas kernels, on_device(): pl.pallas_call(kernel, out_shape=(jax.ShapeDtypeStruct((16 * CAP, T, T),...  109 us
    pallas_call x1, Pallas kernels, on_device(): pl.pallas_call(unpack, out_shape=jax.ShapeDtypeStruct((1, 32, T, T), bf16...  2.5 us

profile of v2, /device:TPU:1, one launch (start us, length us, event | category | flops | bytes accessed | tf_op | source)
XLA Modules:
  0.0 111.6 jit_solution(8111688734339299577)
XLA Ops:
  0.0 109.1 %shard_map.55 = (bf16[48,128,128]{2,1,0:T(8,128)(2,1)}, s32[8,128]{1,0:T(8,128)}) custom-call(bf16[1024,512]{1,0:T(8,128)(2,1)} %a_hbm.1, bf16[1024,512]{1,0:T(8,128)(2,1)} %b_hbm.1, s32[4,8]{1,0:T(4,128)} %bitcast.3, s32[4,8]{1,0:T(4,128)} %bitcast.4, s32[4,8]{1,0:T(4,128)} %bitcast.5), custom_call_target="tpu_custom_call" | custom-call | flops 8589934592 | bytes 4194304 | tf_op jit(solution)/shard_map/pallas_call | solution.py:329
  109.1 2.5 %shard_map.56 = bf16[1,32,128,128]{3,2,1,0:T(8,128)(2,1)} custom-call(s32[8,128]{1,0:T(8,128)} %get-tuple-element.7.slots, bf16[48,128,128]{2,1,0:T(8,128)(2,1)} %get-tuple-element.8.arrived), custom_call_target="tpu_custom_call" | custom-call | tf_op jit(solution)/shard_map/pallas_call | solution.py:364

commit v3 on v2

--- a/solution.py
+++ b/solution.py
@@ -10,8 +10,8 @@
 MESH = pl.DeviceIdType.MESH
 T = 128
 CAP = 3
-PIECES = 4
-LATE = 0
+PIECES = 8
+LATE = 1
 GREET_ALL = False
 SPREAD = [1, 15, 2, 14, 3, 13, 4, 12, 5, 11, 6, 10, 7, 9, 8]
 PARTS = 2

time: 112 us -> 108 us (0.964)
  Pallas kernels: 112 us -> 108 us
    pallas_call x1, Pallas kernels: 109 us -> 105 us  [on_device(): pl.pallas_call(kernel, out_shape=(jax.ShapeDtypeStruct((16 * CAP, T, T),...]
where the time goes in v3:
time: 108 us
  Pallas kernels  108 us (100%)
    pallas_call x1, Pallas kernels, on_device(): pl.pallas_call(kernel, out_shape=(jax.ShapeDtypeStruct((16 * CAP, T, T),...  105 us
    pallas_call x1, Pallas kernels, on_device(): pl.pallas_call(unpack, out_shape=jax.ShapeDtypeStruct((1, 32, T, T), bf16...  2.5 us

profile of v3, /device:TPU:1, one launch (start us, length us, event | category | flops | bytes accessed | tf_op | source)
XLA Modules:
  0.0 108.0 jit_solution(14977079678952882418)
XLA Ops:
  0.0 105.5 %shard_map.55 = (bf16[48,128,128]{2,1,0:T(8,128)(2,1)}, s32[8,128]{1,0:T(8,128)}) custom-call(bf16[1024,512]{1,0:T(8,128)(2,1)} %a_hbm.1, bf16[1024,512]{1,0:T(8,128)(2,1)} %b_hbm.1, s32[4,8]{1,0:T(4,128)} %bitcast.3, s32[4,8]{1,0:T(4,128)} %bitcast.4, s32[4,8]{1,0:T(4,128)} %bitcast.5), custom_call_target="tpu_custom_call" | custom-call | flops 8589934592 | bytes 4194304 | tf_op jit(solution)/shard_map/pallas_call | solution.py:329
  105.5 2.5 %shard_map.56 = bf16[1,32,128,128]{3,2,1,0:T(8,128)(2,1)} custom-call(s32[8,128]{1,0:T(8,128)} %get-tuple-element.7.slots, bf16[48,128,128]{2,1,0:T(8,128)(2,1)} %get-tuple-element.8.arrived), custom_call_target="tpu_custom_call" | custom-call | tf_op jit(solution)/shard_map/pallas_call | solution.py:364

commit v4 on v3

--- a/solution.py
+++ b/solution.py
@@ -12,9 +12,8 @@
 CAP = 3
 PIECES = 8
 LATE = 1
-GREET_ALL = False
 SPREAD = [1, 15, 2, 14, 3, 13, 4, 12, 5, 11, 6, 10, 7, 9, 8]
-PARTS = 2
+PARTS = ((0, 32), (32, 80), (80, 128))
 
 
 class Sems:
@@ -111,38 +110,33 @@
         ).wait_recv()
 
     barrier = pltpu.get_barrier_semaphore()
-    if GREET_ALL:
-        peers = [(row, lax.rem(col + d, 16)) for d in range(1, 16)]
-    else:
-        peers = [(row, col_of(1, 0, 0)), (row, col_of(-1, 0, 0)), (row, col_of(0, 1, 0)), (row, col_of(0, 0, 1))]
+    peers = [(row, col_of(1, 0, 0)), (row, col_of(-1, 0, 0)), (row, col_of(0, 1, 0)), (row, col_of(0, 0, 1))]
     peers += [(row_of(1, 0), col), (row_of(-1, 0), col), (row_of(0, 1), col)]
     for peer in peers:
         pl.semaphore_signal(barrier, inc=1, device_id=peer, device_id_type=MESH)
 
-    rows_p = 8 // PIECES
     order = own_order()
     loads = []
     for n, p in enumerate(order):
-        rows = pl.ds(p * rows_p * T, rows_p * T)
+        thin = pl.ds(p * 16, 16)
         loads.append((
-            pltpu.make_async_copy(a_hbm.at[rows], a_in.at[rows], local_sem.at[2 + 2 * n]),
-            pltpu.make_async_copy(b_hbm.at[rows], b_in.at[rows], local_sem.at[3 + 2 * n]),
+            pltpu.make_async_copy(a_hbm.at[:, thin], a_in.at[:, thin], local_sem.at[2 + 2 * n]),
+            pltpu.make_async_copy(b_hbm.at[p], b_in.at[p], local_sem.at[3 + 2 * n]),
         ))
         for load in loads[-1]:
             load.start()
 
-    def mask(src, tile_flags, dst, p):
-        for i in range(p * rows_p, (p + 1) * rows_p):
-            for j in range(4):
-                flag = tile_flags[j, i].astype(jnp.float32)
-                block = src[pl.ds(i * T, T), pl.ds(j * T, T)].astype(jnp.float32) * flag
-                dst[i, :, pl.ds(j * T, T)] = block.astype(jnp.bfloat16)
+    def mask(src, tile_flags, dst, i, rows):
+        for j in range(4):
+            flag = tile_flags[j, i].astype(jnp.float32)
+            block = src[i, rows, pl.ds(j * T, T)].astype(jnp.float32) * flag
+            dst[i, rows, pl.ds(j * T, T)] = block.astype(jnp.bfloat16)
 
     def a_piece(dx, dv, dc, p):
-        return a_all.at[col_of(-dx, dv, dc), pl.ds(p * rows_p, rows_p)]
+        return a_all.at[col_of(-dx, dv, dc), :, pl.ds(p * 16, 16)]
 
     def b_piece(dy, dv, p):
-        return b_all.at[row_of(-dy, dv), pl.ds(p * rows_p, rows_p)]
+        return b_all.at[row_of(-dy, dv), p]
 
     def send_a(dx, dv, p, how):
         piece = a_piece(dx, dv, 0, p)
@@ -172,8 +166,9 @@
         late = p >= PIECES - LATE
         for load in loads[n]:
             load.wait()
-        mask(a_in, a_tiles, mine_a, p)
-        mask(b_in, b_tiles, mine_b, p)
+        for i in range(8):
+            mask(a_in, a_tiles, mine_a, i, pl.ds(p * 16, 16))
+        mask(b_in, b_tiles, mine_b, p, pl.ds(0, T))
         if n == 0:
             pl.semaphore_wait(barrier, len(peers))
         for one in (send_a, send_b):
@@ -209,43 +204,49 @@
 
     odd = lax.rem(x + y, 2)
     near, far = lax.rem(x + 1, 4), lax.rem(x + 3, 4)
-    size = T // PARTS
-
-    def dots(quarter, v, part):
-        result = None
-        for c in range(2):
-            left = a_all[quarter * 4 + v * 2 + c, :, pl.ds(part * size, size), :].reshape(8 * size, 4 * T)
-            right = b_all[quarter * 2 + v, pl.ds(c * 4, 4)].reshape(4 * T, 4 * T)
-            term = jnp.dot(left, right, preferred_element_type=jnp.float32)
-            result = term if result is None else result + term
+
+    def dots(result, quarters, rows, k_tiles):
+        count = rows[1] - rows[0]
+        for quarter in quarters:
+            for v in range(2):
+                for c in range(2):
+                    k = [t - 4 * c for t in k_tiles if t // 4 == c]
+                    if not k:
+                        continue
+                    left = a_all[quarter * 4 + v * 2 + c, :, rows[0]:rows[1], k[0] * T:(k[-1] + 1) * T]
+                    right = b_all[quarter * 2 + v, 4 * c + k[0]:4 * c + k[-1] + 1]
+                    term = jnp.dot(
+                        left.reshape(8 * count, len(k) * T), right.reshape(len(k) * T, 4 * T),
+                        preferred_element_type=jnp.float32,
+                    )
+                    result = term if result is None else result + term
         return result
 
-    def add_dots(opposite, part):
-        def quarters(one, other):
-            result = total[part] if opposite else None
-            for quarter in (one, other):
-                for v in range(2):
-                    term = dots(quarter, v, part)
-                    result = term if result is None else result + term
-            total[part] = result
-
-        @pl.when(odd == 0)
-        def _():
-            quarters(*((x, lax.rem(x + 2, 4)) if opposite else (near, far)))
-
-        @pl.when(odd == 1)
-        def _():
-            quarters(*((lax.rem(x + 2, 4), lax.rem(y + 2, 4)) if opposite else (x, y)))
+    early_quarters = ((near, far), (x, y))
+    last_quarters = ((x, lax.rem(x + 2, 4)), (lax.rem(x + 2, 4), lax.rem(y + 2, 4)))
+
+    def for_parity(step):
+        for parity in range(2):
+            @pl.when(odd == parity)
+            def _():
+                total[...] = step(early_quarters[parity], last_quarters[parity])
 
     todo = {(m, steps, dv, p) for m in "abs" for steps in range(4) for dv in range(2) for p in range(PIECES)}
-    todo -= {("a", 0, 0, p) for p in range(PIECES)} | {("b", 0, 0, p) for p in range(PIECES)}
-
-    def need(steps, dv):
-        for p in range(PIECES):
-            if ("s", steps, dv, p) in todo:
-                todo.discard(("s", steps, dv, p))
-                got_s(steps, dv, p)
-
+    todo -= {(m, 0, 0, p) for p in range(PIECES) for m in "ab"}
+
+    def of_part(part, steps):
+        lo, hi = part
+        return {("a", d, dv, p) for d in steps for dv in range(2) for p in range(lo // 16, hi // 16)}
+
+    def need(part, steps):
+        for _, d, dv, p in sorted(of_part(part, steps)):
+            if ("s", d, dv, p) in todo:
+                todo.discard(("s", d, dv, p))
+                landed(a_piece(d, dv, 1, p), recv_s.at[d, dv, p], (row, col_of(0, 0, 1)))
+
+    head, late_k = PARTS[0], range(PIECES - LATE, PIECES)
+    early_k = range(PIECES - LATE)
+    early_set = of_part(head, (0, 1, 3)) | {("b", d, dv, p) for d in (0, 1, 3) for dv in range(2) for p in early_k}
     early = False
     for m, steps, dv, p in arrival_order():
         todo.discard((m, steps, dv, p))
@@ -257,58 +258,58 @@
             (send_a if m == "a" else send_b)(steps, dv, p, how)
         if m == "a":
             send_a(steps, dv, p, "core")
-        if not early and not any(n != "s" and d != 2 for n, d, _, _ in todo):
+        if not early and not early_set & todo:
             early = True
             for d in range(1, 16):
                 peer = lax.rem(col + d, 16)
                 send(label_out.at[peer], label_in.at[col], recv_l.at[d], (row, peer))
             label_in[col] = label_out[col]
-            for dx in (0, 1, 3):
-                for dv in range(2):
-                    need(dx, dv)
-            for part in range(PARTS):
-                add_dots(False, part)
+            need(head, (0, 1, 3))
+            for_parity(lambda first, last: dots(None, first, head, early_k))
 
     for d in range(1, 16):
         peer = lax.rem(col - d + 16, 16)
         landed(label_in.at[peer], recv_l.at[d], (row, peer))
     slots_ref[...] = jnp.clip(jnp.sum(label_in[...], axis=0) - 1, 0, 16 * CAP - 1)
 
-    for dv in range(2):
-        need(2, dv)
-
     stays = []
-    for part in range(PARTS):
-        add_dots(True, part)
-        ladder = total[part].astype(jnp.bfloat16).reshape(8, size, 4 * T)
+    for n, part in enumerate(PARTS):
+        need(part, range(4))
+        lo, hi = part
+        if n == 0:
+            for_parity(lambda first, last: dots(dots(total[...], first, part, late_k), last, part, range(8)))
+            ladder = total[...]
+        else:
+            ladder = dots(None, range(4), part, range(8))
+        ladder = ladder.astype(jnp.bfloat16).reshape(8, hi - lo, 4 * T)
         for i in range(8):
             for j in range(4):
-                tiles[part, i * 4 + j] = ladder[i, :, j * T:(j + 1) * T]
+                tiles[i * 4 + j, lo:hi] = ladder[i, :, j * T:(j + 1) * T]
 
         def pack(k, carry):
-            packed_parts[part][k] = tiles[part, jnp.clip(table_s[0, k], 0, 31)]
+            packed_parts[n][k] = tiles[jnp.clip(table_s[0, k], 0, 31), lo:hi]
             return carry
 
         lax.fori_loop(0, 16 * CAP, pack, 0, unroll=4)
-        rows = pl.ds(part * size, size)
+        rows = pl.ds(lo, hi - lo)
         for d in SPREAD:
             peer = lax.rem(col + d, 16)
             send(
-                packed_parts[part].at[pl.ds(peer * CAP, CAP)], arrived.at[pl.ds(col * CAP, CAP), rows],
-                recv_d.at[part, d], (row, peer),
+                packed_parts[n].at[pl.ds(peer * CAP, CAP)], arrived.at[pl.ds(col * CAP, CAP), rows],
+                recv_d.at[n, d], (row, peer),
             )
         stays.append(pltpu.make_async_copy(
-            packed_parts[part].at[pl.ds(col * CAP, CAP)], arrived.at[pl.ds(col * CAP, CAP), rows],
-            local_sem.at[2 + part],
+            packed_parts[n].at[pl.ds(col * CAP, CAP)], arrived.at[pl.ds(col * CAP, CAP), rows],
+            local_sem.at[2 + n],
         ))
         stays[-1].start()
 
-    for part in range(PARTS):
-        rows = pl.ds(part * size, size)
-        stays[part].wait()
+    for n, (lo, hi) in enumerate(PARTS):
+        rows = pl.ds(lo, hi - lo)
+        stays[n].wait()
         for d in SPREAD:
             peer = lax.rem(col - d + 16, 16)
-            landed(arrived.at[pl.ds(peer * CAP, CAP), rows], recv_d.at[part, d], (row, peer))
+            landed(arrived.at[pl.ds(peer * CAP, CAP), rows], recv_d.at[n, d], (row, peer))
     for copy in started:
         copy.wait_send()
 
@@ -323,7 +324,6 @@
 
 def on_device(integrals, amplitudes, integral_tiles, amplitude_tiles, targets):
     bf16 = jnp.bfloat16
-    size = T // PARTS
     vmem, smem, hbm = (pl.BlockSpec(memory_space=s) for s in (pltpu.VMEM, pltpu.SMEM, pl.ANY))
     dma = pltpu.SemaphoreType.DMA
     arrived, slots = pl.pallas_call(
@@ -335,13 +335,13 @@
         in_specs=[hbm, hbm, smem, smem, smem],
         out_specs=(hbm, vmem),
         scratch_shapes=[
-            pltpu.VMEM((8 * T, 4 * T), bf16),
-            pltpu.VMEM((8 * T, 4 * T), bf16),
+            pltpu.VMEM((8, T, 4 * T), bf16),
+            pltpu.VMEM((8, T, 4 * T), bf16),
             pltpu.VMEM((16, 8, T, 4 * T), bf16),
             pltpu.VMEM((8, 8, T, 4 * T), bf16),
-            pltpu.VMEM((PARTS, 8 * size, 4 * T), jnp.float32),
-            pltpu.VMEM((PARTS, 32, size, T), bf16),
-            [pltpu.VMEM((16 * CAP, size, T), bf16) for _ in range(PARTS)],
+            pltpu.VMEM((8 * PARTS[0][1], 4 * T), jnp.float32),
+            pltpu.VMEM((32, T, T), bf16),
+            [pltpu.VMEM((16 * CAP, hi - lo, T), bf16) for lo, hi in PARTS],
             pltpu.VMEM((16, 8, 128), jnp.int32),
             pltpu.VMEM((16, 8, 128), jnp.int32),
             pltpu.VMEM((1, 8, 128), jnp.int32),
@@ -351,7 +351,7 @@
             dma((4, 2, PIECES)),
             dma((4, 2, PIECES)),
             dma((16,)),
-            dma((PARTS, 16)),
+            dma((len(PARTS), 16)),
             dma((2 + 2 * PIECES,)),
         ],
         compiler_params=pltpu.CompilerParams(
@@ -360,7 +360,7 @@
         cost_estimate=pl.CostEstimate(
             flops=2 * 1024 * 512 * 8192, bytes_accessed=4 * 2**20, transcendentals=0
         ),
-    )(integrals, amplitudes, integral_tiles.T, amplitude_tiles.T, targets.T)
+    )(integrals.reshape(8, T, 4 * T), amplitudes.reshape(8, T, 4 * T), integral_tiles.T, amplitude_tiles.T, targets.T)
     return pl.pallas_call(
         unpack,
         out_shape=jax.ShapeDtypeStruct((1, 32, T, T), bf16),

time: 108 us -> 104 us (0.963)
  Pallas kernels: 108 us -> 104 us
    pallas_call x1, Pallas kernels: 105 us -> 101 us  [on_device(): pl.pallas_call(kernel, out_shape=(jax.ShapeDtypeStruct((16 * CAP, T, T),...]
where the time goes in v4:
time: 104 us
  Pallas kernels  104 us (100%)
    pallas_call x1, Pallas kernels, on_device(): pl.pallas_call(kernel, out_shape=(jax.ShapeDtypeStruct((16 * CAP, T, T),...  101 us
    pallas_call x1, Pallas kernels, on_device(): pl.pallas_call(unpack, out_shape=jax.ShapeDtypeStruct((1, 32, T, T), bf16...  2.5 us

profile of v4, /device:TPU:1, one launch (start us, length us, event | category | flops | bytes accessed | tf_op | source)
XLA Modules:
  0.0 103.8 jit_solution(15329367759363604003)
XLA Ops:
  0.0 101.3 %shard_map.55 = (bf16[48,128,128]{2,1,0:T(8,128)(2,1)}, s32[8,128]{1,0:T(8,128)}) custom-call(bf16[8,128,512]{2,1,0:T(8,128)(2,1)} %bitcast.5, bf16[8,128,512]{2,1,0:T(8,128)(2,1)} %bitcast.6, s32[4,8]{1,0:T(4,128)} %bitcast.7, s32[4,8]{1,0:T(4,128)} %bitcast.8, s32[4,8]{1,0:T(4,128)} %bitcast.9), custom_call_target="tpu_custom_call" | custom-call | flops 8589934592 | bytes 4194304 | tf_op jit(solution)/shard_map/pallas_call | solution.py:329
  101.3 2.5 %shard_map.56 = bf16[1,32,128,128]{3,2,1,0:T(8,128)(2,1)} custom-call(s32[8,128]{1,0:T(8,128)} %get-tuple-element.7.slots, bf16[48,128,128]{2,1,0:T(8,128)(2,1)} %get-tuple-element.8.arrived), custom_call_target="tpu_custom_call" | custom-call | tf_op jit(solution)/shard_map/pallas_call | solution.py:364

commit v5 on v4

--- a/solution.py
+++ b/solution.py
@@ -25,40 +25,47 @@
         return self.ref.at[self.used - 1]
 
 
+def halved(steps, dv, p):
+    return LATE == 1 and steps in (1, 3) and dv == 1 and p == PIECES // 2 - 1
+
+
 def forwards(steps, dv, p):
-    kept = (p < PIECES // 2) != (dv == 1 and PIECES - LATE == p)
-    return steps == 1 and kept or steps == 3 and not kept
+    return halved(steps, dv, p) or (steps == 1) == (p < PIECES // 2)
 
 
 def arrival_order():
     queues = {(m, way): [] for m in "ab" for way in ("left", "right", "z")}
-    left_over, order, now = {key: 0.0 for key in queues}, [], 0.0
+    left_over, order, halves = {key: 0.0 for key in queues}, [], set()
     for m in "ab":
         for p in own_order():
-            queues[m, "left"].append((3, 0, p))
-            queues[m, "right"].append((1, 0, p))
+            queues[m, "left"].append((3, 0, p, 1))
+            queues[m, "right"].append((1, 0, p, 1))
         for p in own_order():
             if p < PIECES - LATE:
-                queues[m, "z"].append((0, 1, p))
+                queues[m, "z"].append((0, 1, p, 1))
         for p in range(PIECES - LATE, PIECES):
-            queues[m, "z"].append((0, 1, p))
+            queues[m, "z"].append((0, 1, p, 1))
     while any(queues.values()):
         both = queues["a", "z"] and queues["b", "z"]
         for (m, way), queue in queues.items():
             if queue:
                 left_over[m, way] += 0.0625 if way == "z" and both else 0.125
         for (m, way), queue in queues.items():
-            if queue and left_over[m, way] >= 1.0:
+            if queue and left_over[m, way] >= queue[0][3]:
                 left_over[m, way] = 0.0
-                steps, dv, p = queue.pop(0)
+                steps, dv, p, size = queue.pop(0)
+                if size < 1 and (m, steps, dv, p) not in halves:
+                    halves.add((m, steps, dv, p))
+                    continue
                 order.append((m, steps, dv, p))
+                size = 0.5 if halved(steps, dv, p) else 1
                 for how in onward(steps, dv, p):
                     if how == "z":
-                        queues[m, "z"].append((steps, 1 - dv, p))
+                        queues[m, "z"].append((steps, 1 - dv, p, 1))
                     elif how == "right":
-                        queues[m, "right"].append((steps + 1, dv, p))
+                        queues[m, "right"].append((steps + 1, dv, p, size))
                     else:
-                        queues[m, "left"].append(((steps + 3) % 4, dv, p))
+                        queues[m, "left"].append(((steps + 3) % 4, dv, p, size))
     return order
 
 
@@ -81,7 +88,7 @@
 def kernel(
     a_hbm, b_hbm, a_tiles, b_tiles, targets, arrived, slots_ref,
     a_in, b_in, a_all, b_all, total, tiles, packed_parts, label_out, label_in, table, table_s,
-    send_ref, recv_a, recv_s, recv_b, recv_l, recv_d, local_sem,
+    send_ref, recv_a, recv_s, recv_b, recv_h, recv_l, recv_d, local_sem,
 ):
     row, col = lax.axis_index("row"), lax.axis_index("col")
     y, zh = row // 2, row % 2
@@ -138,8 +145,18 @@
     def b_piece(dy, dv, p):
         return b_all.at[row_of(-dy, dv), p]
 
+    def a_half(dx, dv, p, h):
+        return a_all.at[col_of(-dx, dv, 0), pl.ds(4 * h, 4), pl.ds(p * 16, 16)]
+
+    def b_half(dy, dv, p, h):
+        return b_all.at[row_of(-dy, dv), p, pl.ds(T // 2 * h, T // 2)]
+
     def send_a(dx, dv, p, how):
         piece = a_piece(dx, dv, 0, p)
+        if halved(dx, dv, p) and how in ("left", "right"):
+            h, side = (0, 1) if how == "right" else (1, -1)
+            send(a_half(dx, dv, p, h), a_half(dx, dv, p, h), recv_h.at[0, h], (row, col_of(side, 0, 0)))
+            return
         if how == "right":
             send(piece, piece, recv_a.at[dx + 1, dv, p], (row, col_of(1, 0, 0)))
         elif how == "left":
@@ -151,6 +168,10 @@
 
     def send_b(dy, dv, p, how):
         piece = b_piece(dy, dv, p)
+        if halved(dy, dv, p) and how in ("left", "right"):
+            h, side = (0, 1) if how == "right" else (1, -1)
+            send(b_half(dy, dv, p, h), b_half(dy, dv, p, h), recv_h.at[1, h], (row_of(side, 0), col))
+            return
         if how == "right":
             send(piece, piece, recv_b.at[dy + 1, dv, p], (row_of(1, 0), col))
         elif how == "left":
@@ -250,7 +271,13 @@
     early = False
     for m, steps, dv, p in arrival_order():
         todo.discard((m, steps, dv, p))
-        if m == "a":
+        if steps == 2 and halved(1, dv, p):
+            for h in range(2):
+                if m == "a":
+                    landed(a_half(2, dv, p, h), recv_h.at[0, h], (row, col_of(0, 1, 0)))
+                else:
+                    landed(b_half(2, dv, p, h), recv_h.at[1, h], (row_of(0, 1), col))
+        elif m == "a":
             landed(a_piece(steps, dv, 0, p), recv_a.at[steps, dv, p], (row, col_of(0, 1, 0)))
         else:
             landed(b_piece(steps, dv, p), recv_b.at[steps, dv, p], (row_of(0, 1), col))
@@ -267,11 +294,6 @@
             need(head, (0, 1, 3))
             for_parity(lambda first, last: dots(None, first, head, early_k))
 
-    for d in range(1, 16):
-        peer = lax.rem(col - d + 16, 16)
-        landed(label_in.at[peer], recv_l.at[d], (row, peer))
-    slots_ref[...] = jnp.clip(jnp.sum(label_in[...], axis=0) - 1, 0, 16 * CAP - 1)
-
     stays = []
     for n, part in enumerate(PARTS):
         need(part, range(4))
@@ -303,6 +325,11 @@
             local_sem.at[2 + n],
         ))
         stays[-1].start()
+
+    for d in range(1, 16):
+        peer = lax.rem(col - d + 16, 16)
+        landed(label_in.at[peer], recv_l.at[d], (row, peer))
+    slots_ref[...] = jnp.clip(jnp.sum(label_in[...], axis=0) - 1, 0, 16 * CAP - 1)
 
     for n, (lo, hi) in enumerate(PARTS):
         rows = pl.ds(lo, hi - lo)
@@ -350,6 +377,7 @@
             dma((4, 2, PIECES)),
             dma((4, 2, PIECES)),
             dma((4, 2, PIECES)),
+            dma((2, 2)),
             dma((16,)),
             dma((len(PARTS), 16)),
             dma((2 + 2 * PIECES,)),

time: 104 us -> 102 us (0.981)
  Pallas kernels: 104 us -> 102 us
    pallas_call x1, Pallas kernels: 101 us -> 99.6 us  [on_device(): pl.pallas_call(kernel, out_shape=(jax.ShapeDtypeStruct((16 * CAP, T, T),...]
where the time goes in v5:
time: 102 us
  Pallas kernels  102 us (100%)
    pallas_call x1, Pallas kernels, on_device(): pl.pallas_call(kernel, out_shape=(jax.ShapeDtypeStruct((16 * CAP, T, T),...  99.6 us
    pallas_call x1, Pallas kernels, on_device(): pl.pallas_call(unpack, out_shape=jax.ShapeDtypeStruct((1, 32, T, T), bf16...  2.5 us

profile of v5, /device:TPU:1, one launch (start us, length us, event | category | flops | bytes accessed | tf_op | source)
XLA Modules:
  0.0 102.1 jit_solution(1812588581526751622)
XLA Ops:
  0.0 99.6 %shard_map.55 = (bf16[48,128,128]{2,1,0:T(8,128)(2,1)}, s32[8,128]{1,0:T(8,128)}) custom-call(bf16[8,128,512]{2,1,0:T(8,128)(2,1)} %bitcast.5, bf16[8,128,512]{2,1,0:T(8,128)(2,1)} %bitcast.6, s32[4,8]{1,0:T(4,128)} %bitcast.7, s32[4,8]{1,0:T(4,128)} %bitcast.8, s32[4,8]{1,0:T(4,128)} %bitcast.9), custom_call_target="tpu_custom_call" | custom-call | flops 8589934592 | bytes 4194304 | tf_op jit(solution)/shard_map/pallas_call | solution.py:356
  99.6 2.5 %shard_map.56 = bf16[1,32,128,128]{3,2,1,0:T(8,128)(2,1)} custom-call(s32[8,128]{1,0:T(8,128)} %get-tuple-element.7.slots, bf16[48,128,128]{2,1,0:T(8,128)(2,1)} %get-tuple-element.8.arrived), custom_call_target="tpu_custom_call" | custom-call | tf_op jit(solution)/shard_map/pallas_call | solution.py:392

commit v6 on v5

--- a/solution.py
+++ b/solution.py
@@ -268,7 +268,10 @@
     head, late_k = PARTS[0], range(PIECES - LATE, PIECES)
     early_k = range(PIECES - LATE)
     early_set = of_part(head, (0, 1, 3)) | {("b", d, dv, p) for d in (0, 1, 3) for dv in range(2) for p in early_k}
-    early = False
+    soon_k, rest_k = (0, 1, 4), (2, 3, 5, 6, 7)
+    soon_set = of_part(head, range(4)) | {("b", 2, dv, p) for dv in range(2) for p in soon_k}
+    soon_set |= {("b", d, dv, p) for d in (0, 1, 3) for dv in range(2) for p in range(PIECES)}
+    early = soon = False
     for m, steps, dv, p in arrival_order():
         todo.discard((m, steps, dv, p))
         if steps == 2 and halved(1, dv, p):
@@ -293,13 +296,17 @@
             label_in[col] = label_out[col]
             need(head, (0, 1, 3))
             for_parity(lambda first, last: dots(None, first, head, early_k))
+        if early and not soon and not soon_set & todo:
+            soon = True
+            need(head, (2,))
+            for_parity(lambda first, last: dots(dots(total[...], first, head, late_k), last, head, soon_k))
 
     stays = []
     for n, part in enumerate(PARTS):
         need(part, range(4))
         lo, hi = part
         if n == 0:
-            for_parity(lambda first, last: dots(dots(total[...], first, part, late_k), last, part, range(8)))
+            for_parity(lambda first, last: dots(total[...], last, part, rest_k))
             ladder = total[...]
         else:
             ladder = dots(None, range(4), part, range(8))

time: 102 us -> 102 us (level)
  no operation moved by 1% of the time
where the time goes in v6:
time: 102 us
  Pallas kernels  102 us (100%)
    pallas_call x1, Pallas kernels, on_device(): pl.pallas_call(kernel, out_shape=(jax.ShapeDtypeStruct((16 * CAP, T, T),...  99.6 us
    pallas_call x1, Pallas kernels, on_device(): pl.pallas_call(unpack, out_shape=jax.ShapeDtypeStruct((1, 32, T, T), bf16...  2.5 us

profile of v6, /device:TPU:1, one launch (start us, length us, event | category | flops | bytes accessed | tf_op | source)
XLA Modules:
  0.0 102.1 jit_solution(9177652538777935134)
XLA Ops:
  0.0 99.6 %shard_map.55 = (bf16[48,128,128]{2,1,0:T(8,128)(2,1)}, s32[8,128]{1,0:T(8,128)}) custom-call(bf16[8,128,512]{2,1,0:T(8,128)(2,1)} %bitcast.5, bf16[8,128,512]{2,1,0:T(8,128)(2,1)} %bitcast.6, s32[4,8]{1,0:T(4,128)} %bitcast.7, s32[4,8]{1,0:T(4,128)} %bitcast.8, s32[4,8]{1,0:T(4,128)} %bitcast.9), custom_call_target="tpu_custom_call" | custom-call | flops 8589934592 | bytes 4194304 | tf_op jit(solution)/shard_map/pallas_call | solution.py:363
  99.6 2.5 %shard_map.56 = bf16[1,32,128,128]{3,2,1,0:T(8,128)(2,1)} custom-call(s32[8,128]{1,0:T(8,128)} %get-tuple-element.7.slots, bf16[48,128,128]{2,1,0:T(8,128)(2,1)} %get-tuple-element.8.arrived), custom_call_target="tpu_custom_call" | custom-call | tf_op jit(solution)/shard_map/pallas_call | solution.py:399
